TPU v7x, 32 devices: a whole 2x2x4 slice. The times are simulated.
32 devices in a mesh: groups: 2 (over y), grid: 4 (over z), feat: 4 (over x, core).
Axes of the slice: x: 2, y: 2, z: 4, core: 2. Of those that a mesh axis runs over, the one named last changes fastest.
Arguments:
- grid_state: bfloat16 [8192, 227], P(('groups', 'grid')), parts along dimension 0, may hold values from -6 to 6
- mesh_state: bfloat16 [2048, 512], P('grid', 'feat'), may hold values from -6 to 6
- enc_rows: int32 [4, 4, 32], P('grid'), may hold values from 0 to 1023
- enc_targets: int32 [4, 4, 32], P('grid'), may hold values from 0 to 512, as said below
- mesh_senders: int32 [16384], P('grid'), may hold values from 0 to 639
- mesh_receivers: int32 [16384], P('grid'), may hold values from 0 to 511
- dec_rows: int32 [4, 4, 64], P('grid'), may hold values from 0 to 511
- dec_targets: int32 [4, 4, 64], P('grid'), may hold values from 0 to 1024, as said below
- enc_grid_w: bfloat16 [227, 512], P(None, 'feat'), may hold values from -0.375 to 0.375
- enc_mesh_w: bfloat16 [512, 512], P(None, 'feat'), may hold values from -0.25 to 0.25
- enc_bias: float32 [512], P('feat'), may hold values from -3 to 3
- enc_out_w: bfloat16 [512, 512], P('feat'), may hold values from -0.25 to 0.25
- enc_gain: float32 [512], P('feat'), may hold values from 0.1 to 1.9
- proc_send_w: bfloat16 [2, 512, 512], P(None, None, 'feat'), may hold values from -0.25 to 0.25
- proc_recv_w: bfloat16 [2, 512, 512], P(None, None, 'feat'), may hold values from -0.25 to 0.25
- proc_bias: float32 [2, 512], P(None, 'feat'), may hold values from -3 to 3
- proc_out_w: bfloat16 [2, 512, 512], P(None, 'feat'), may hold values from -0.25 to 0.25
- proc_gain: float32 [2, 512], P(None, 'feat'), may hold values from 0.1 to 1.9
- dec_mesh_w: bfloat16 [512, 512], P(None, 'feat'), may hold values from -0.25 to 0.25
- dec_grid_w: bfloat16 [227, 512], P(None, 'feat'), may hold values from -0.375 to 0.375
- dec_bias: float32 [512], P('feat'), may hold values from -3 to 3
- dec_out_w: bfloat16 [512, 227], P('feat'), may hold values from -0.25 to 0.25
Outputs:
- next_state: float32 [8192, 227], P(('groups', 'grid', 'feat')), parts along dimension 0
There are 2 independent parts, one for each index of `groups`. A program takes and returns all parts, laid end to end along the dimension named above; an argument that names none is the same for every part. Nothing has to cross between parts.
Inputs may be any that keep to these rules, and one draw needn't show every extreme that they name: `enc_targets`: value 512 marks an empty slot; in each partition pair the filled slots come first; one mesh partition has all 32 slots filled from every grid partition. `dec_targets`: value 1024 marks an empty slot; in each partition pair the filled slots come first; one grid partition has all 64 slots filled from every mesh partition.
All inputs are finite; a program needn't handle non-finite values.
Results may differ from a plain program's by a relative error of at most 0.009.
Values may be sent and summed in bfloat16 or wider, within the bound.
A program may use at most 64 MiB of HBM per device.

v0:
```python
import jax
import jax.numpy as jnp
from jax import lax
from jax.sharding import PartitionSpec as P

D = 512
HALO = 64


def padded(cells, sides, width):
    for axis, dim in sides:
        count = lax.axis_size(axis)
        head = lax.slice_in_dim(cells, 0, width, axis=dim)
        tail = lax.slice_in_dim(cells, cells.shape[dim] - width, cells.shape[dim], axis=dim)
        cells = jnp.concatenate(
            [
                lax.ppermute(tail, axis, [(i, (i + 1) % count) for i in range(count)]),
                cells,
                lax.ppermute(head, axis, [((i + 1) % count, i) for i in range(count)]),
            ],
            axis=dim,
        )
    return cells


def one_hot(index, count):
    return (index[:, None] == jnp.arange(count, dtype=jnp.int32)[None, :]).astype(jnp.bfloat16)


def project(latent, weights):
    latent_bf = latent.astype(jnp.bfloat16)
    shard_part = lax.all_gather(latent_bf, "feat", axis=1, tiled=True)
    totals = tuple(
        (jnp.dot(shard_part, weight, preferred_element_type=jnp.float32) for weight in weights)
    )
    return tuple((running.astype(jnp.bfloat16) for running in totals))


def update(latent, summed, out_weight, scales):
    partial_sums = jnp.dot(summed, out_weight, preferred_element_type=jnp.float32)
    blended = lax.psum_scatter(
        partial_sums.astype(jnp.bfloat16), "feat", scatter_dimension=1, tiled=True
    ).astype(jnp.float32)
    row_sum, row_squares = lax.psum(
        (jnp.sum(blended, axis=1), jnp.sum(blended * blended, axis=1)), "feat"
    )
    centre = row_sum / D
    spread = row_squares / D - centre * centre
    return latent + scales * ((blended - centre[:, None]) * lax.rsqrt(spread + 1e-05)[:, None])


def aggregate(slot_proj, targets, table, bias):
    flat_targets = targets.reshape(-1)
    flat_proj = slot_proj.reshape(-1, slot_proj.shape[-1])
    selector = one_hot(flat_targets, table.shape[0])
    picked = jnp.dot(selector, table, preferred_element_type=jnp.float32)
    hidden = jax.nn.silu(flat_proj.astype(jnp.float32) + picked + bias).astype(jnp.bfloat16)
    return jnp.einsum("sm,sh->mh", selector, hidden, preferred_element_type=jnp.float32).astype(
        jnp.bfloat16
    )


def local(
    grid_state,
    mesh_state,
    enc_rows,
    enc_targets,
    mesh_senders,
    mesh_receivers,
    dec_rows,
    dec_targets,
    enc_grid_w,
    enc_mesh_w,
    enc_bias,
    enc_out_w,
    enc_gain,
    proc_send_w,
    proc_recv_w,
    proc_bias,
    proc_out_w,
    proc_gain,
    dec_mesh_w,
    dec_grid_w,
    dec_bias,
    dec_out_w,
):
    feat_count = lax.axis_size("feat")
    feat_index = lax.axis_index("feat")
    latent = mesh_state.astype(jnp.float32)
    (mesh_proj,) = project(latent, (enc_mesh_w,))
    grid_proj = jnp.dot(grid_state, enc_grid_w, preferred_element_type=jnp.float32).astype(
        jnp.bfloat16
    )
    outgoing = jnp.take(grid_proj, enc_rows[0], axis=0)
    slot_proj, full_targets = (
        lax.all_to_all(outgoing, "grid", split_axis=0, concat_axis=0, tiled=True),
        lax.all_to_all(enc_targets[0], "grid", split_axis=0, concat_axis=0, tiled=True),
    )
    summed = aggregate(slot_proj, full_targets, mesh_proj, enc_bias)
    latent = update(latent, summed, enc_out_w, enc_gain)
    for layer_at in range(proc_send_w.shape[0]):
        send_proj, recv_proj = project(latent, (proc_send_w[layer_at], proc_recv_w[layer_at]))
        widened = padded(send_proj, (("grid", 0),), HALO)
        from_senders = jnp.dot(
            one_hot(mesh_senders, widened.shape[0]), widened, preferred_element_type=jnp.float32
        )
        selector = one_hot(mesh_receivers, recv_proj.shape[0])
        from_receivers = jnp.dot(selector, recv_proj, preferred_element_type=jnp.float32)
        hidden = jax.nn.silu(from_senders + from_receivers + proc_bias[layer_at]).astype(
            jnp.bfloat16
        )
        summed = jnp.einsum(
            "sm,sh->mh", selector, hidden, preferred_element_type=jnp.float32
        ).astype(jnp.bfloat16)
        latent = update(latent, summed, proc_out_w[layer_at], proc_gain[layer_at])
    (mesh_out,) = project(latent, (dec_mesh_w,))
    outgoing = jnp.take(mesh_out, dec_rows[0], axis=0)
    arrived, arrived_targets = (
        lax.all_to_all(outgoing, "grid", split_axis=0, concat_axis=0, tiled=True),
        lax.all_to_all(dec_targets[0], "grid", split_axis=0, concat_axis=0, tiled=True),
    )
    grid_rows = grid_state.shape[0]
    grid_query = jnp.dot(grid_state, dec_grid_w, preferred_element_type=jnp.float32).astype(
        jnp.bfloat16
    )
    flat_targets = arrived_targets.reshape(-1)
    picked = jnp.take(grid_query, jnp.minimum(flat_targets, grid_rows - 1), axis=0)
    flat_arrived = arrived.reshape(-1, arrived.shape[-1])
    hidden = jax.nn.silu(
        flat_arrived.astype(jnp.float32) + picked.astype(jnp.float32) + dec_bias
    ).astype(jnp.bfloat16)
    summed = jax.ops.segment_sum(
        hidden.astype(jnp.float32), flat_targets, num_segments=grid_rows + 1
    )[:grid_rows].astype(jnp.bfloat16)
    quarter_rows = grid_rows // feat_count
    own_rows = lax.dynamic_slice_in_dim(
        grid_state, feat_index * quarter_rows, quarter_rows, 0
    ).astype(jnp.float32)
    regrouped = lax.all_to_all(summed, "feat", split_axis=0, concat_axis=1, tiled=True)
    whole_out_rows = lax.all_gather(dec_out_w, "feat", axis=0, tiled=True)
    return own_rows + jnp.dot(regrouped, whole_out_rows, preferred_element_type=jnp.float32)


def solution(mesh):
    in_specs = (
        P(("groups", "grid"), None),
        P("grid", "feat"),
        P("grid", None, None),
        P("grid", None, None),
        P("grid"),
        P("grid"),
        P("grid", None, None),
        P("grid", None, None),
        P(None, "feat"),
        P(None, "feat"),
        P("feat"),
        P("feat", None),
        P("feat"),
        P(None, None, "feat"),
        P(None, None, "feat"),
        P(None, "feat"),
        P(None, "feat", None),
        P(None, "feat"),
        P(None, "feat"),
        P(None, "feat"),
        P("feat"),
        P("feat", None),
    )
    out_specs = P(("groups", "grid", "feat"), None)
    return jax.shard_map(local, mesh=mesh, in_specs=in_specs, out_specs=out_specs, check_vma=False)
```

profile of v0, /device:TPU:1, one launch (start us, length us, event | category | flops | bytes accessed | tf_op | source)
XLA Modules:
  0.0 210.7 jit_solution(671869334549598406)
XLA Ops:
  6.5 5.6 %all-to-all-start.1 = ((s32[4,1,32]{2,1,0:T(1,128)}), s32[4,1,32]{2,1,0:T(1,128)S(1)}, u32[]{:S(2)}, u32[]{:S(2)}) async-start(s32[4,1,32]{2,1,0:T(1,128)} %bitcast.97), calls=%async_computation.1 | async-start | bytes 4096 | tf_op jit(solution)/shard_map/all_to_all | solution.py:97
  12.1 0.7 compare_select_fusion.2
  12.8 0.7 compare_and_fusion.1
  13.5 0.1 reshape.131
  13.6 1.4 convolution_convert_fusion.4
  14.9 0.7 gather_fusion
  15.7 0.7 broadcast_select_fusion.1
  16.4 4.5 %all-to-all-start.2 = ((bf16[4,32,128]{2,1,0:T(8,128)(2,1)}), bf16[4,32,128]{2,1,0:T(8,128)(2,1)S(1)}, u32[]{:S(2)}, u32[]{:S(2)}) async-start(bf16[4,32,128]{2,1,0:T(8,128)(2,1)} %broadcast_select_fusion.1), calls=%async_computation.2 | async-start | bytes 65536 | tf_op jit(solution)/shard_map/all_to_all | solution.py:96
  20.9 8.9 %all_gather.15 = bf16[512,512]{1,0:T(8,128)(2,1)S(1)} all-gather(bf16[512,128]{1,0:T(8,128)(2,1)} %param.23), channel_id=1, replica_groups=mesh['groups'=2,'grid'=4,'feat'=4] {'feat'}, dimensions={1}, use_global_device_ids=true | all-gather | bytes 655360 | tf_op jit(solution)/shard_map/all_gather | solution.py:32
  29.8 0.6 broadcast.155
  30.4 0.7 reduce.13
  31.1 0.1 eq.20
  31.2 1.4 multiply_convert_fusion.4
  32.7 0.5 convolution_convert_fusion.2
  33.2 1.0 copy.26
  34.3 22.0 %reduce-scatter.10.cloned.1.call-done = bf16[128,512]{1,0:T(8,128)(2,1)} async-done(((bf16[512,512]{1,0:T(8,128)(2,1)}), bf16[128,512]{1,0:T(8,128)(2,1)}) %reduce-scatter.10.cloned.1.call-update) | async-done | bytes 131088
  56.3 1.0 copy.27
  57.3 0.2 convert_reduce_fusion.2
  57.5 5.7 %all-reduce.2 = (f32[512]{0:T(512)S(1)}, f32[512]{0:T(512)S(1)}) all-reduce(f32[512]{0:T(512)S(1)} %get-tuple-element.10, f32[512]{0:T(512)S(1)} %get-tuple-element.9), channel_id=1, replica_groups=mesh['groups'=2,'grid'=4,'feat'=4] {'feat'}, use_global_device_ids=true, to_apply=%region_4.5 | all-reduce | flops 1024 | bytes 8192 | tf_op jit(solution)/shard_map/psum | solution.py:44
  63.2 0.2 fusion.36
  63.5 7.9 %all_gather.16 = bf16[512,512]{1,0:T(8,128)(2,1)S(1)} all-gather(bf16[512,128]{1,0:T(8,128)(2,1)S(1)} %fusion.36), channel_id=1, replica_groups=mesh['groups'=2,'grid'=4,'feat'=4] {'feat'}, dimensions={1}, use_global_device_ids=true | all-gather | bytes 655360 | tf_op jit(solution)/shard_map/all_gather | solution.py:32
  71.4 0.3 convolution_convert_fusion.9
  71.7 1.3 collective-permute-start
  73.0 2.0 collective-permute-start.1
  75.0 3.2 %fusion.5 = f32[4096,128]{1,0:T(8,128)} fusion(s32[4096]{0:T(1024)S(1)} %copy-done.15, bf16[512,512]{1,0:T(8,128)(2,1)S(1)} %all_gather.16, bf16[2,512,128]{2,1,0:T(8,128)(2,1)S(1)} %copy-done.12), kind=kOutput, calls=%fused_computation.11 | convolution fusion | flops 606142464 | bytes 2768896 | tf_op jit(solution)/shard_map/dot_general | solution.py:108
  78.2 4.8 %multiply_convert_fusion.1 = bf16[4096,128]{1,0:T(8,128)(2,1)S(1)} fusion(f32[4096,128]{1,0:T(8,128)} %fusion.5, s32[4096]{0:T(1024)S(1)} %copy-done.14, f32[128]{0:T(128)S(1)} %get-tuple-element.35, bf16[64,128]{1,0:T(8,128)(2,1)S(1)} %collective-permute-done.1, bf16[512,128]{1,0:T(8,128)(2,1)S(1)} %convolution_convert_fusion.9, ...), kind=kOutput, calls=%fused_computation.23 | convolution fusion | flops 677871616 | bytes 3326464 | tf_op jit(solution)/shard_map/dot_general | solution.py:104
  83.0 3.2 %convolution_convert_fusion.1 = bf16[512,512]{1,0:T(8,128)(2,1)S(1)} fusion(bf16[4096,128]{1,0:T(8,128)(2,1)S(1)} %multiply_convert_fusion.1, s32[4096]{0:T(1024)S(1)} %copy-done.15, bf16[2,128,512]{2,1,0:T(8,128)(2,1)S(1)} %copy-done.13), kind=kOutput, calls=%fused_computation.25 | convolution fusion | flops 606404608 | bytes 1720320 | tf_op jit(solution)/shard_map/dot_general | solution.py:40
  86.2 1.0 copy.28
  87.3 3.2 %all-to-all-start = ((s32[4,1,64]{2,1,0:T(1,128)}), s32[4,1,64]{2,1,0:T(1,128)S(1)}, u32[]{:S(2)}, u32[]{:S(2)}) async-start(s32[4,1,64]{2,1,0:T(1,128)} %bitcast), calls=%async_computation | async-start | bytes 4096 | tf_op jit(solution)/shard_map/all_to_all | solution.py:120
  90.6 17.8 %reduce-scatter.12.cloned.1.call-done = bf16[128,512]{1,0:T(8,128)(2,1)} async-done(((bf16[512,512]{1,0:T(8,128)(2,1)}), bf16[128,512]{1,0:T(8,128)(2,1)}) %reduce-scatter.12.cloned.1.call-update) | async-done | bytes 131088
  108.4 1.0 copy.29
  109.4 0.2 convert_reduce_fusion.1
  109.6 5.7 %all-reduce.1 = (f32[512]{0:T(512)S(1)}, f32[512]{0:T(512)S(1)}) all-reduce(f32[512]{0:T(512)S(1)} %get-tuple-element.8, f32[512]{0:T(512)S(1)} %get-tuple-element.7), channel_id=1, replica_groups=mesh['groups'=2,'grid'=4,'feat'=4] {'feat'}, use_global_device_ids=true, to_apply=%region_9.10 | all-reduce | flops 1024 | bytes 8192 | tf_op jit(solution)/shard_map/psum | solution.py:44
  115.3 0.3 fusion.77
  115.7 7.9 %all_gather.17 = bf16[512,512]{1,0:T(8,128)(2,1)S(1)} all-gather(bf16[512,128]{1,0:T(8,128)(2,1)S(1)} %get-tuple-element.19), channel_id=1, replica_groups=mesh['groups'=2,'grid'=4,'feat'=4] {'feat'}, dimensions={1}, use_global_device_ids=true | all-gather | bytes 655360 | tf_op jit(solution)/shard_map/all_gather | solution.py:32
  123.6 0.3 convolution_convert_fusion.7
  123.9 1.3 collective-permute-start.2
  125.2 2.0 collective-permute-start.3
  127.3 3.2 %fusion.3 = f32[4096,128]{1,0:T(8,128)} fusion(s32[4096]{0:T(1024)S(1)} %copy-done.15, bf16[512,512]{1,0:T(8,128)(2,1)S(1)} %all_gather.17, bf16[2,512,128]{2,1,0:T(8,128)(2,1)S(1)} %copy-done.12), kind=kOutput, calls=%fused_computation.9 | convolution fusion | flops 606142464 | bytes 2768896 | tf_op jit(solution)/shard_map/dot_general | solution.py:108
  130.5 4.7 %multiply_convert_fusion = bf16[4096,128]{1,0:T(8,128)(2,1)S(1)} fusion(f32[4096,128]{1,0:T(8,128)} %fusion.3, s32[4096]{0:T(1024)S(1)} %copy-done.14, f32[128]{0:T(128)S(1)} %get-tuple-element.34, bf16[64,128]{1,0:T(8,128)(2,1)S(1)} %collective-permute-done.3, bf16[512,128]{1,0:T(8,128)(2,1)S(1)} %convolution_convert_fusion.7, ...), kind=kOutput, calls=%fused_computation.22 | convolution fusion | flops 677871616 | bytes 3326464 | tf_op jit(solution)/shard_map/dot_general | solution.py:104
  135.2 3.2 %convolution_convert_fusion = bf16[512,512]{1,0:T(8,128)(2,1)S(1)} fusion(bf16[4096,128]{1,0:T(8,128)(2,1)S(1)} %multiply_convert_fusion, s32[4096]{0:T(1024)S(1)} %copy-done.15, bf16[2,128,512]{2,1,0:T(8,128)(2,1)S(1)} %copy-done.13), kind=kOutput, calls=%fused_computation.24 | convolution fusion | flops 606404608 | bytes 1720320 | tf_op jit(solution)/shard_map/dot_general | solution.py:40
  138.4 1.0 copy.30
  139.5 0.1 reshape.139
  139.6 0.4 convolution_convert_fusion.3
  140.0 0.7 fusion.76
  140.7 0.1 reshape.165
  140.7 0.1 min.26
  140.9 19.7 %reduce-scatter.14.cloned.1.call-done = bf16[128,512]{1,0:T(8,128)(2,1)} async-done(((bf16[512,512]{1,0:T(8,128)(2,1)}), bf16[128,512]{1,0:T(8,128)(2,1)}) %reduce-scatter.14.cloned.1.call-update) | async-done | bytes 131088
  160.6 1.0 copy.31
  161.6 0.2 convert_reduce_fusion
  161.8 5.7 %all-reduce = (f32[512]{0:T(512)S(1)}, f32[512]{0:T(512)S(1)}) all-reduce(f32[512]{0:T(512)S(1)} %get-tuple-element.6, f32[512]{0:T(512)S(1)} %get-tuple-element.5), channel_id=1, replica_groups=mesh['groups'=2,'grid'=4,'feat'=4] {'feat'}, use_global_device_ids=true, to_apply=%region_14.15 | all-reduce | flops 1024 | bytes 8192 | tf_op jit(solution)/shard_map/psum | solution.py:44
  167.5 0.2 fusion.34
  167.8 8.0 %all_gather.18 = bf16[512,512]{1,0:T(8,128)(2,1)S(1)} all-gather(bf16[512,128]{1,0:T(8,128)(2,1)S(1)} %fusion.34), channel_id=1, replica_groups=mesh['groups'=2,'grid'=4,'feat'=4] {'feat'}, dimensions={1}, use_global_device_ids=true | all-gather | bytes 655360 | tf_op jit(solution)/shard_map/all_gather | solution.py:32
  175.8 0.3 convolution_convert_fusion.5
  176.1 0.9 gather_fusion.1
  177.0 0.7 broadcast_select_fusion
  177.7 4.3 %all-to-all-start.3 = ((bf16[4,64,128]{2,1,0:T(8,128)(2,1)}), bf16[4,64,128]{2,1,0:T(8,128)(2,1)S(1)}, u32[]{:S(2)}, u32[]{:S(2)}) async-start(bf16[4,64,128]{2,1,0:T(8,128)(2,1)} %broadcast_select_fusion), calls=%async_computation.3 | async-start | bytes 131072 | tf_op jit(solution)/shard_map/all_to_all | solution.py:119
  182.0 4.6 %all-to-all-done.3 = bf16[4,64,128]{2,1,0:T(8,128)(2,1)S(1)} async-done(((bf16[4,64,128]{2,1,0:T(8,128)(2,1)}), bf16[4,64,128]{2,1,0:T(8,128)(2,1)S(1)}, u32[]{:S(2)}, u32[]{:S(2)}) %all-to-all-start.3) | async-done | bytes 65568 | tf_op jit(solution)/shard_map/all_to_all | solution.py:119
  186.6 2.7 %scatter_custom_fusion = f32[1025,128]{1,0:T(8,128)S(1)} fusion(s32[256]{0:T(256)S(1)} %reshape.155, f32[]{:T(128)} %constant.64.clone.1, bf16[256,128]{1,0:T(8,128)(2,1)S(1)} %bitcast.88, f32[]{:T(128)} %constant.69.clone.1, f32[128]{0:T(128)S(1)} %copy-done.11, pred[256]{0:T(512)(128)(4,1)S(1)} %compare_and_fusion, bf16[]{:T(256)} %constant.68.clone.1, ...), kind=kCustom, calls=%fused_computation.52 | custom fusion | flops 393216 | bytes 857610 | tf_op jit(solution)/shard_map/scatter-add | solution.py:132
  189.3 0.7 slice.107
  190.1 4.9 %all-to-all-start.4 = ((bf16[4,256,128]{2,1,0:T(8,128)(2,1)}), bf16[4,256,128]{2,1,0:T(8,128)(2,1)S(1)}, u32[]{:S(2)}, u32[]{:S(2)}) async-start(bf16[4,256,128]{2,1,0:T(8,128)(2,1)} %bitcast.22), calls=%async_computation.4 | async-start | bytes 524288 | tf_op jit(solution)/shard_map/all_to_all | solution.py:139
  195.0 8.0 %all_gather.19 = bf16[512,227]{0,1:T(8,128)(2,1)S(1)} all-gather(bf16[128,227]{0,1:T(8,128)(2,1)S(1)} %copy-done.5), channel_id=1, replica_groups=mesh['groups'=2,'grid'=4,'feat'=4] {'feat'}, dimensions={0}, use_global_device_ids=true | all-gather | bytes 290560 | tf_op jit(solution)/shard_map/all_gather | solution.py:140
  203.0 0.1 copy.25
  203.2 0.9 convolution_add_fusion
  (61 shorter events, 0.5 us)
Async XLA Ops:
  6.5 26.1 %copy-start = (bf16[128,512]{1,0:T(8,128)(2,1)S(1)}, bf16[128,512]{1,0:T(8,128)(2,1)}, u32[]{:S(2)}) copy-start(bf16[128,512]{1,0:T(8,128)(2,1)} %param.33) | copy-start | bytes 393220
  6.5 9.9 %all-to-all-start.1 = ((s32[4,1,32]{2,1,0:T(1,128)}), s32[4,1,32]{2,1,0:T(1,128)S(1)}, u32[]{:S(2)}, u32[]{:S(2)}) async-start(s32[4,1,32]{2,1,0:T(1,128)} %bitcast.97), calls=%async_computation.1 | async-start | bytes 4096 | tf_op jit(solution)/shard_map/all_to_all | solution.py:97
  15.7 18.6 %copy-start.9 = (f32[2,128]{1,0:T(2,128)S(1)}, f32[2,128]{1,0:T(2,128)}, u32[]{:S(2)}) copy-start(f32[2,128]{1,0:T(2,128)} %param.37) | copy-start | bytes 3076
  16.4 14.8 %all-to-all-start.2 = ((bf16[4,32,128]{2,1,0:T(8,128)(2,1)}), bf16[4,32,128]{2,1,0:T(8,128)(2,1)S(1)}, u32[]{:S(2)}, u32[]{:S(2)}) async-start(bf16[4,32,128]{2,1,0:T(8,128)(2,1)} %broadcast_select_fusion.1), calls=%async_computation.2 | async-start | bytes 65536 | tf_op jit(solution)/shard_map/all_to_all | solution.py:96
  20.9 42.3 %copy-start.2 = (bf16[512,128]{1,0:T(8,128)(2,1)S(1)}, bf16[512,128]{1,0:T(8,128)(2,1)}, u32[]{:S(2)}) copy-start(bf16[512,128]{1,0:T(8,128)(2,1)} %param.23) | copy-start | bytes 393220
  20.9 42.3 %copy-start.8 = (f32[128]{0:T(128)S(1)}, f32[128]{0:T(128)}, u32[]{:S(2)}) copy-start(f32[128]{0:T(128)} %param.34) | copy-start | bytes 1540
  20.9 35.4 %reduce-scatter.10.cloned.1.call-start = ((), (), s32[]{:S(2)}) async-start(), calls=%async_computation.8 | async-start | bytes 655360
  32.6 38.7 %copy-start.3 = (bf16[2,512,128]{2,1,0:T(8,128)(2,1)S(1)}, bf16[2,512,128]{2,1,0:T(8,128)(2,1)}, u32[]{:S(2)}) copy-start(bf16[2,512,128]{2,1,0:T(8,128)(2,1)} %param.35) | copy-start | bytes 786436
  33.2 41.8 %copy-start.12 = (bf16[2,512,128]{2,1,0:T(8,128)(2,1)S(1)}, bf16[2,512,128]{2,1,0:T(8,128)(2,1)}, u32[]{:S(2)}) copy-start(bf16[2,512,128]{2,1,0:T(8,128)(2,1)} %param.36) | copy-start | bytes 786436
  33.2 41.8 %copy-start.15 = (s32[4096]{0:T(1024)S(1)}, s32[4096]{0:T(1024)}, u32[]{:S(2)}) copy-start(s32[4096]{0:T(1024)} %param.27) | copy-start | bytes 49156
  34.2 74.2 %reduce-scatter.12.cloned.1.call-start = ((), (), s32[]{:S(2)}) async-start(), calls=%async_computation.9 | async-start | bytes 655360
  71.7 6.5 %collective-permute-start = (bf16[64,128]{1,0:T(8,128)(2,1)S(1)}, bf16[64,128]{1,0:T(8,128)(2,1)S(1)}, u32[]{:S(2)}, u32[]{:S(2)}) collective-permute-start(bf16[64,128]{1,0:T(8,128)(2,1)S(1)} %get-tuple-element.23), channel_id=1, source_target_pairs={{0,4},{4,8},{8,12},{12,0},{1,5},{5,9},{9,13},{13,1},{2,6},{6,10},{... | collective-permute-start | bytes 49160 | tf_op jit(solution)/shard_map/ppermute | solution.py:17
  73.0 5.2 %copy-start.14 = (s32[4096]{0:T(1024)S(1)}, s32[4096]{0:T(1024)}, u32[]{:S(2)}) copy-start(s32[4096]{0:T(1024)} %param.26) | copy-start | bytes 49156
  73.0 5.2 %collective-permute-start.1 = (bf16[64,128]{1,0:T(8,128)(2,1)S(1)}, bf16[64,128]{1,0:T(8,128)(2,1)S(1)}, u32[]{:S(2)}, u32[]{:S(2)}) collective-permute-start(bf16[64,128]{1,0:T(8,128)(2,1)S(1)} %get-tuple-element.24), channel_id=1, source_target_pairs={{4,0},{8,4},{12,8},{0,12},{5,1},{9,5},{13,9},{1,13},{6,2},{10,6},{... | collective-permute-start | bytes 49160 | tf_op jit(solution)/shard_map/ppermute | solution.py:19
  78.2 4.8 %copy-start.13 = (bf16[2,128,512]{2,1,0:T(8,128)(2,1)S(1)}, bf16[2,128,512]{2,1,0:T(8,128)(2,1)}, u32[]{:S(2)}) copy-start(bf16[2,128,512]{2,1,0:T(8,128)(2,1)} %param.38) | copy-start | bytes 786436
  83.0 7.6 %copy-start.10 = (f32[2,128]{1,0:T(2,128)S(1)}, f32[2,128]{1,0:T(2,128)}, u32[]{:S(2)}) copy-start(f32[2,128]{1,0:T(2,128)} %param.39) | copy-start | bytes 3076
  83.0 7.6 %copy-start.7 = (s32[1,4,64]{2,1,0:T(4,128)S(1)}, s32[1,4,64]{2,1,0:T(4,128)}, u32[]{:S(2)}) copy-start(s32[1,4,64]{2,1,0:T(4,128)} %param.28) | copy-start | bytes 3076
  87.3 52.7 %all-to-all-start = ((s32[4,1,64]{2,1,0:T(1,128)}), s32[4,1,64]{2,1,0:T(1,128)S(1)}, u32[]{:S(2)}, u32[]{:S(2)}) async-start(s32[4,1,64]{2,1,0:T(1,128)} %bitcast), calls=%async_computation | async-start | bytes 4096 | tf_op jit(solution)/shard_map/all_to_all | solution.py:120
  90.5 70.1 %reduce-scatter.14.cloned.1.call-start = ((), (), s32[]{:S(2)}) async-start(), calls=%async_computation.10 | async-start | bytes 655360
  123.9 6.6 %collective-permute-start.2 = (bf16[64,128]{1,0:T(8,128)(2,1)S(1)}, bf16[64,128]{1,0:T(8,128)(2,1)S(1)}, u32[]{:S(2)}, u32[]{:S(2)}) collective-permute-start(bf16[64,128]{1,0:T(8,128)(2,1)S(1)} %get-tuple-element.21), channel_id=1, source_target_pairs={{0,4},{4,8},{8,12},{12,0},{1,5},{5,9},{9,13},{13,1},{2,6},{6,10},{... | collective-permute-start | bytes 49160 | tf_op jit(solution)/shard_map/ppermute | solution.py:17
  125.2 5.2 %collective-permute-start.3 = (bf16[64,128]{1,0:T(8,128)(2,1)S(1)}, bf16[64,128]{1,0:T(8,128)(2,1)S(1)}, u32[]{:S(2)}, u32[]{:S(2)}) collective-permute-start(bf16[64,128]{1,0:T(8,128)(2,1)S(1)} %get-tuple-element.22), channel_id=1, source_target_pairs={{4,0},{8,4},{12,8},{0,12},{5,1},{9,5},{13,9},{1,13},{6,2},{10,6},{... | collective-permute-start | bytes 49160 | tf_op jit(solution)/shard_map/ppermute | solution.py:19
  135.2 4.4 %copy-start.1 = (bf16[1024,227]{0,1:T(8,128)(2,1)S(1)}, bf16[1024,227]{0,1:T(8,128)(2,1)}, u32[]{:S(2)}) copy-start(bf16[1024,227]{0,1:T(8,128)(2,1)} %param.22) | copy-start | bytes 1394692
  135.2 4.4 %copy-start.6 = (bf16[227,128]{1,0:T(8,128)(2,1)S(1)}, bf16[227,128]{1,0:T(8,128)(2,1)}, u32[]{:S(2)}) copy-start(bf16[227,128]{1,0:T(8,128)(2,1)} %param.41) | copy-start | bytes 174340
  138.4 37.4 %copy-start.4 = (bf16[512,128]{1,0:T(8,128)(2,1)S(1)}, bf16[512,128]{1,0:T(8,128)(2,1)}, u32[]{:S(2)}) copy-start(bf16[512,128]{1,0:T(8,128)(2,1)} %param.40) | copy-start | bytes 393220
  139.5 47.2 %copy-start.11 = (f32[128]{0:T(128)S(1)}, f32[128]{0:T(128)}, u32[]{:S(2)}) copy-start(f32[128]{0:T(128)} %param.42) | copy-start | bytes 1540
  167.8 27.3 %copy-start.5 = (bf16[128,227]{0,1:T(8,128)(2,1)S(1)}, bf16[128,227]{0,1:T(8,128)(2,1)}, u32[]{:S(2)}) copy-start(bf16[128,227]{0,1:T(8,128)(2,1)} %param.43) | copy-start | bytes 174340
  177.7 8.9 %all-to-all-start.3 = ((bf16[4,64,128]{2,1,0:T(8,128)(2,1)}), bf16[4,64,128]{2,1,0:T(8,128)(2,1)S(1)}, u32[]{:S(2)}, u32[]{:S(2)}) async-start(bf16[4,64,128]{2,1,0:T(8,128)(2,1)} %broadcast_select_fusion), calls=%async_computation.3 | async-start | bytes 131072 | tf_op jit(solution)/shard_map/all_to_all | solution.py:119
  190.1 13.0 %all-to-all-start.4 = ((bf16[4,256,128]{2,1,0:T(8,128)(2,1)}), bf16[4,256,128]{2,1,0:T(8,128)(2,1)S(1)}, u32[]{:S(2)}, u32[]{:S(2)}) async-start(bf16[4,256,128]{2,1,0:T(8,128)(2,1)} %bitcast.22), calls=%async_computation.4 | async-start | bytes 524288 | tf_op jit(solution)/shard_map/all_to_all | solution.py:139
Sparse Core Ops, SparseCore 0:
  34.4 21.9 reduce-scatter.9
  87.4 20.9 reduce-scatter.11
  139.6 20.9 reduce-scatter.13
where the time goes:
time: 212 us; the launch traced here: 211 us
  waiting for transfers between devices  64.2 us (30%)
  blocking collectives  57.9 us (27%)
  starting transfers between devices  29.3 us (14%)
  matrix products  27.8 us (13%)
  between operations  13.5 us (6%)
  local copies, waits for them, and re-layouts  9.7 us (5%)
  other arithmetic  8.29 us (4%)
    unnamed x6, waiting for transfers between devices  59.5 us
    all_gather x4, blocking collectives, project(): shard_part = lax.all_gather(latent_bf, 'feat', axis=1, tiled=True)  32.8 us
    psum x3, blocking collectives, update(): lax.psum((jnp.sum(blended, axis=1), jnp.sum(blended * blended, axis=1)),...  17.1 us
    dot_general x2, matrix products, local(): jnp.dot(one_hot(mesh_senders, widened.shape[0]), widened, preferred_eleme...  9.48 us
    all_to_all x2, starting transfers between devices, local(): lax.all_to_all(outgoing, 'grid', split_axis=0, concat_axis=0, tiled=True)  8.81 us
    all_gather x1, blocking collectives, local(): whole_out_rows = lax.all_gather(dec_out_w, 'feat', axis=0, tiled=True)  8.01 us
    dot_general x3, matrix products, update(): jnp.dot(summed, out_weight, preferred_element_type=jnp.float32)  6.91 us
    dot_general x2, matrix products, local(): jnp.dot(selector, recv_proj, preferred_element_type=jnp.float32)  6.41 us
  transfers between devices with their start and end apart: 12, of which 4 were waited for; matrix products, arithmetic and copies ran while one was open for 11% of the time, Pallas kernels for 0%

commit v1 on v0

v1 whole, which is shorter than its diff:
```python
import functools

import jax
import jax.numpy as jnp
from jax import lax
from jax.experimental import pallas as pl
from jax.experimental.pallas import tpu as pltpu
from jax.sharding import PartitionSpec as P

HALO = 64
BF = jnp.bfloat16
F32 = jnp.float32
EDGE_TILE = 128
EDGE_BLOCK = 512
MESH = pl.DeviceIdType.MESH


def repeat(count, body):
    if count <= 4:
        for i in range(count):
            body(i)
    else:

        def step(i, carry):
            body(i)
            return carry

        lax.fori_loop(0, count, step, 0)


def as_column(row):
    n = row.shape[1]
    diagonal = lax.broadcasted_iota(jnp.int32, (n, n), 0) == lax.broadcasted_iota(
        jnp.int32, (n, n), 1
    )
    spread = jnp.where(diagonal, jnp.broadcast_to(row.astype(F32), (n, n)), 0.0)
    return jnp.sum(spread, axis=1, keepdims=True)


def hits(index, count, offset):
    lanes = lax.broadcasted_iota(jnp.int32, (index.shape[0], count), 1) + offset
    wide = jnp.broadcast_to(index[:, :1], (index.shape[0], count))
    return jnp.where(wide == lanes.astype(F32), 1.0, 0.0).astype(BF)


def dot(a, b):
    return jnp.dot(a, b, preferred_element_type=F32)


def dot_t(a, b):
    return lax.dot_general(a, b, (((0,), (0,)), ((), ())), preferred_element_type=F32)


def silu(x):
    half = 0.5 * x
    return half + half * jnp.tanh(half)


def kernel(
    n_grid,
    n_feat,
    grid_state,
    mesh_state,
    enc_rows,
    enc_targets,
    senders,
    receivers,
    dec_rows,
    dec_targets,
    enc_grid_w,
    enc_mesh_w,
    enc_bias,
    enc_out_w,
    enc_gain,
    proc_send_w,
    proc_recv_w,
    proc_bias,
    proc_out_w,
    proc_gain,
    dec_mesh_w,
    dec_grid_w,
    dec_bias,
    dec_out_w,
    out,
    state_all,
    gain_all,
    out_w_all,
    dec_w_all,
    sums_all,
    dec_all,
    enc_out_slots,
    enc_out_index,
    dec_out_slots,
    dec_out_index,
    enc_in_slots,
    enc_in_index,
    dec_in_slots,
    dec_in_index,
    dec_pick,
    dec_query,
    dec_spread,
    gather_sel,
    scatter_sel,
    pre,
    table,
    halo,
    latent,
    latent_bf,
    send_sem,
    recv_sem,
):
    z = lax.axis_index("grid")
    f = lax.axis_index("feat")
    side = f + 1 - 2 * (f % 2)
    cross = (f + 2) % n_feat
    layers = proc_send_w.shape[0]
    nodes, part = mesh_state.shape
    grid_rows = grid_state.shape[0]
    cap, cap2 = enc_rows.shape[2], dec_rows.shape[2]
    edges = senders.shape[0] * EDGE_TILE
    sems = [0]
    sent = []

    def new_sem(count=1):
        sems[0] += count
        return sems[0] - count

    def send(src, dst, sem, where):
        return pltpu.make_async_remote_copy(
            src_ref=src,
            dst_ref=dst,
            send_sem=send_sem.at[sem],
            recv_sem=recv_sem.at[sem],
            device_id=where,
            device_id_type=MESH,
        )

    def columns(index):
        return pl.ds(pl.multiple_of(index * part, part), part)

    class Gather:
        def __init__(self, ref, by_rows, pieces):
            self.ref, self.by_rows = ref, by_rows
            size = (part if by_rows else ref.shape[0]) // pieces
            self.direct = send(self.at(f), self.at(f), new_sem(), {"feat": side})
            self.over, self.forward = [], []
            for k in range(pieces):
                here, there = self.at(f, k, size), self.at(cross, k, size)
                self.over.append(send(here, here, new_sem(), {"feat": cross}))
                self.forward.append(send(there, there, new_sem(), {"feat": side}))

        def at(self, index, k=0, size=None):
            if self.by_rows:
                size = part if size is None else size
                start = pl.multiple_of(index * part + k * size, size)
                return self.ref.at[pl.ds(start, size), :]
            size = self.ref.shape[0] if size is None else size
            return self.ref.at[pl.ds(k * size, size), columns(index)]

        def start(self):
            for copy in self.over:
                copy.start()
            self.direct.start()

        def middle(self):
            for over, forward in zip(self.over, self.forward):
                over.wait_recv()
                forward.start()

        def finish(self):
            self.direct.wait_recv()
            for forward in self.forward:
                forward.wait_recv()
            sent.extend([self.direct] + self.over + self.forward)

    class Exchange:
        def __init__(self, src, dst, size):
            self.src, self.dst, self.size = src, dst, size
            self.sem = new_sem(n_grid)

        def block(self, ref, index):
            return ref.at[pl.ds(pl.multiple_of(index * self.size, self.size), self.size), :]

        def copy(self, step):
            to = (z + step) % n_grid
            return send(
                self.block(self.src, to), self.block(self.dst, z), self.sem + step, {"grid": to}
            )

        def start(self):
            repeat(n_grid - 1, lambda i: self.copy(i + 1).start())
            self.block(self.dst, z)[...] = self.block(self.src, z)[...]

        def finish(self):
            repeat(n_grid - 1, lambda i: self.copy(i + 1).wait_recv())

        def end(self):
            repeat(n_grid - 1, lambda i: self.copy(i + 1).wait_send())

    barrier = pltpu.get_barrier_semaphore()
    for partner in (side, cross):
        pl.semaphore_signal(barrier, inc=1, device_id={"feat": partner}, device_id_type=MESH)
    repeat(
        n_grid - 1,
        lambda i: pl.semaphore_signal(
            barrier, inc=1, device_id={"grid": (z + i + 1) % n_grid}, device_id_type=MESH
        ),
    )

    state_all[:, columns(f)] = mesh_state[...]
    gain_all[:, columns(f)] = jnp.concatenate(
        [enc_gain[...], proc_gain[...], jnp.zeros((7 - layers, part), F32)], axis=0
    )
    out_w_all[0, columns(f), :] = enc_out_w[...]
    for layer in range(layers):
        out_w_all[1 + layer, columns(f), :] = proc_out_w[layer]
    dec_w_all[columns(f), :] = dec_out_w[...]

    state_gather = Gather(state_all, False, 2)
    gain_gather = Gather(gain_all, False, 1)
    weight_gathers = [Gather(out_w_all.at[i], True, 1) for i in range(1 + layers)]
    dec_weight_gather = Gather(dec_w_all, True, 1)
    sum_gathers = [Gather(sums_all.at[i], False, 4) for i in range(1 + layers)]
    dec_gather = Gather(dec_all, False, 2)
    enc_slots = Exchange(enc_out_slots, enc_in_slots, cap)
    enc_index = Exchange(enc_out_index, enc_in_index, cap)
    dec_slots = Exchange(dec_out_slots, dec_in_slots, cap2)
    dec_index = Exchange(dec_out_index, dec_in_index, cap2)

    pl.semaphore_wait(barrier, 2 + n_grid - 1)
    state_gather.start()

    def enc_send(b):
        rows = as_column(enc_rows[0, pl.ds(b, 1), :])
        picked = dot(hits(rows, grid_rows, 0), grid_state[...]).astype(BF)
        where = pl.ds(pl.multiple_of(b * cap, cap), cap)
        enc_out_slots[where, :] = dot(picked, enc_grid_w[...]).astype(BF)
        target = as_column(enc_targets[0, pl.ds(b, 1), :])
        enc_out_index[where, :] = jnp.broadcast_to(target, (cap, 128))

    repeat(n_grid, enc_send)
    enc_slots.start()
    enc_index.start()
    gain_gather.start()
    weight_gathers[0].start()

    def dec_prepare(b):
        where = pl.ds(pl.multiple_of(b * cap2, cap2), cap2)
        target = as_column(dec_targets[0, pl.ds(b, 1), :])
        dec_out_index[where, :] = jnp.broadcast_to(target, (cap2, 128))
        dec_pick[where, :] = hits(as_column(dec_rows[0, pl.ds(b, 1), :]), nodes, 0)

    repeat(n_grid, dec_prepare)
    dec_index.start()
    state_gather.middle()

    def edge_tile(j):
        where = pl.ds(pl.multiple_of(j * EDGE_TILE, EDGE_TILE), EDGE_TILE)
        to_row = receivers[pl.ds(j, 1), :]
        sender, receiver = as_column(senders[pl.ds(j, 1), :]), as_column(to_row)
        gather_sel[where, :nodes] = hits(sender, nodes, HALO)
        gather_sel[where, nodes : 2 * nodes] = hits(receiver, nodes, 0)
        lane = lax.broadcasted_iota(jnp.int32, (EDGE_TILE, 2 * HALO), 1)
        ends = jnp.where(lane < HALO, lane, lane + nodes).astype(F32)
        gather_sel[where, 2 * nodes :] = jnp.where(
            jnp.broadcast_to(sender, ends.shape) == ends, 1.0, 0.0
        ).astype(BF)
        row = lax.broadcasted_iota(jnp.int32, (nodes, EDGE_TILE), 0)
        scatter_sel[:, where] = jnp.where(
            jnp.broadcast_to(to_row, row.shape) == row, 1.0, 0.0
        ).astype(BF)

    def edge_tiles(first, last):
        lax.fori_loop(first, last, lambda j, c: (edge_tile(j), c)[1], 0)

    tiles = edges // EDGE_TILE
    edge_tiles(0, tiles // 2)
    gain_gather.middle()
    weight_gathers[0].middle()

    state_gather.finish()
    mesh_proj = dot(state_all[...], enc_mesh_w[...]).astype(BF)
    enc_slots.finish()
    enc_index.finish()

    total = jnp.zeros((nodes, part), F32)
    chunk = 4 * cap
    for i in range(n_grid // 4):
        where = pl.ds(i * chunk, chunk)
        select = hits(enc_in_index[where, :], nodes, 0)
        before = enc_in_slots[where, :].astype(F32) + dot(select, mesh_proj) + enc_bias[...]
        total += dot_t(select, silu(before).astype(BF))
    sums_all[0, :, columns(f)] = total.astype(BF)
    sum_gathers[0].start()
    edge_tiles(tiles // 2, tiles)

    block = 128

    def update(step):
        gather = sum_gathers[step]
        gather.middle()
        if step == 0:
            gain_gather.finish()
        weight_gathers[step].finish()
        gather.finish()
        for i in range(nodes // block):
            rows = slice(i * block, (i + 1) * block)
            u = dot(sums_all[step, rows, :], out_w_all[step])
            centre = jnp.mean(u, axis=1, keepdims=True)
            spread = jnp.mean(u * u, axis=1, keepdims=True) - centre * centre
            held = state_all[rows, :].astype(F32) if step == 0 else latent[rows, :]
            held += gain_all[step : step + 1, :] * ((u - centre) * lax.rsqrt(spread + 1e-05))
            latent[rows, :] = held
            latent_bf[rows, :] = held.astype(BF)

    update(0)
    right, left = (z + 1) % n_grid, (z + n_grid - 1) % n_grid
    for layer in range(layers):
        table[layer, :nodes, :] = dot(latent_bf[...], proc_send_w[layer]).astype(BF)
        up = send(
            table.at[layer, pl.ds(nodes - HALO, HALO), :],
            halo.at[layer, pl.ds(0, HALO), :],
            new_sem(),
            {"grid": right},
        )
        down = send(
            table.at[layer, pl.ds(0, HALO), :],
            halo.at[layer, pl.ds(HALO, HALO), :],
            new_sem(),
            {"grid": left},
        )
        up.start()
        down.start()
        weight_gathers[1 + layer].start()
        if layer == layers - 1:
            dec_weight_gather.start()
        table[layer, nodes:, :] = dot(latent_bf[...], proc_recv_w[layer]).astype(BF)
        for i in range(edges // EDGE_BLOCK):
            rows = slice(i * EDGE_BLOCK, (i + 1) * EDGE_BLOCK)
            pre[rows, :] = dot(gather_sel[rows, : 2 * nodes], table[layer])
        up.wait_recv()
        down.wait_recv()
        weight_gathers[1 + layer].middle()
        if layer == layers - 1:
            dec_weight_gather.middle()
        total = jnp.zeros((nodes, part), F32)
        for i in range(edges // EDGE_BLOCK):
            rows = slice(i * EDGE_BLOCK, (i + 1) * EDGE_BLOCK)
            before = pre[rows, :] + dot(gather_sel[rows, 2 * nodes :], halo[layer])
            hidden = silu(before + proc_bias[layer : layer + 1, :]).astype(BF)
            total += dot(scatter_sel[:, rows], hidden)
        sums_all[1 + layer, :, columns(f)] = total.astype(BF)
        sum_gathers[1 + layer].start()
        sent.extend([up, down])
        if layer == 0:
            dec_index.finish()
            query = dot(grid_state[...], dec_grid_w[...]).astype(BF)
            quarter = grid_rows // n_feat
            for i in range(n_grid // 4):
                where = pl.ds(i * 4 * cap2, 4 * cap2)
                targets = dec_in_index[where, :]
                dec_query[where, :] = dot(hits(targets, grid_rows, 0), query) + dec_bias[...]
                dec_spread[where, :] = hits(targets, quarter, f * quarter)
        update(1 + layer)

    mesh_out = dot(latent_bf[...], dec_mesh_w[...]).astype(BF)
    for i in range(n_grid // 4):
        where = pl.ds(i * 4 * cap2, 4 * cap2)
        dec_out_slots[where, :] = dot(dec_pick[where, :], mesh_out).astype(BF)
    dec_slots.start()
    dec_slots.finish()
    for i in range(n_grid // 4):
        where = pl.ds(i * 4 * cap2, 4 * cap2)
        before = dec_in_slots[where, :].astype(F32) + dec_query[where, :]
        dec_all[where, columns(f)] = silu(before).astype(BF)
    dec_gather.start()
    dec_weight_gather.finish()
    dec_gather.middle()
    dec_gather.finish()
    quarter = grid_rows // n_feat
    total = jnp.zeros((quarter, part * n_feat), F32)
    for i in range(n_grid // 4):
        where = pl.ds(i * 4 * cap2, 4 * cap2)
        total += dot_t(dec_spread[where, :], dec_all[where, :])
    own = grid_state[pl.ds(pl.multiple_of(f * quarter, quarter), quarter), :]
    out[...] = own.astype(F32) + dot(total.astype(BF), dec_w_all[...])

    for copy in sent:
        copy.wait_send()
    for exchange in (enc_slots, enc_index, dec_slots, dec_index):
        exchange.end()


def local(
    grid_state,
    mesh_state,
    enc_rows,
    enc_targets,
    mesh_senders,
    mesh_receivers,
    dec_rows,
    dec_targets,
    enc_grid_w,
    enc_mesh_w,
    enc_bias,
    enc_out_w,
    enc_gain,
    proc_send_w,
    proc_recv_w,
    proc_bias,
    proc_out_w,
    proc_gain,
    dec_mesh_w,
    dec_grid_w,
    dec_bias,
    dec_out_w,
):
    n_grid, n_feat = lax.axis_size("grid"), lax.axis_size("feat")
    layers = proc_send_w.shape[0]
    nodes, part = mesh_state.shape
    width = part * n_feat
    grid_rows, variables = grid_state.shape
    enc_total = n_grid * enc_rows.shape[2]
    dec_total = n_grid * dec_rows.shape[2]
    edges = mesh_senders.shape[0]
    quarter = grid_rows // n_feat
    sems = 9 * 12 + 2 * layers + 4 * n_grid
    args = (
        grid_state,
        mesh_state,
        enc_rows,
        enc_targets,
        mesh_senders.reshape(-1, EDGE_TILE),
        mesh_receivers.reshape(-1, EDGE_TILE),
        dec_rows,
        dec_targets,
        enc_grid_w,
        enc_mesh_w,
        enc_bias.reshape(1, -1),
        enc_out_w,
        enc_gain.reshape(1, -1),
        proc_send_w,
        proc_recv_w,
        proc_bias,
        proc_out_w,
        proc_gain,
        dec_mesh_w,
        dec_grid_w,
        dec_bias.reshape(1, -1),
        dec_out_w,
    )
    return pl.pallas_call(
        functools.partial(kernel, n_grid, n_feat),
        out_shape=jax.ShapeDtypeStruct((quarter, variables), F32),
        in_specs=[pl.BlockSpec(memory_space=pltpu.VMEM)] * len(args),
        out_specs=pl.BlockSpec(memory_space=pltpu.VMEM),
        scratch_shapes=[
            pltpu.VMEM((nodes, width), BF),
            pltpu.VMEM((8, width), F32),
            pltpu.VMEM((1 + layers, width, width), BF),
            pltpu.VMEM((width, variables), BF),
            pltpu.VMEM((1 + layers, nodes, width), BF),
            pltpu.VMEM((dec_total, width), BF),
            pltpu.VMEM((enc_total, part), BF),
            pltpu.VMEM((enc_total, 128), F32),
            pltpu.VMEM((dec_total, part), BF),
            pltpu.VMEM((dec_total, 128), F32),
            pltpu.VMEM((enc_total, part), BF),
            pltpu.VMEM((enc_total, 128), F32),
            pltpu.VMEM((dec_total, part), BF),
            pltpu.VMEM((dec_total, 128), F32),
            pltpu.VMEM((dec_total, nodes), BF),
            pltpu.VMEM((dec_total, part), F32),
            pltpu.VMEM((dec_total, quarter), BF),
            pltpu.VMEM((edges, 2 * nodes + 2 * HALO), BF),
            pltpu.VMEM((nodes, edges), BF),
            pltpu.VMEM((edges, part), F32),
            pltpu.VMEM((layers, 2 * nodes, part), BF),
            pltpu.VMEM((layers, 2 * HALO, part), BF),
            pltpu.VMEM((nodes, width), F32),
            pltpu.VMEM((nodes, width), BF),
            pltpu.SemaphoreType.DMA((sems,)),
            pltpu.SemaphoreType.DMA((sems,)),
        ],
        compiler_params=pltpu.CompilerParams(
            collective_id=0, has_side_effects=True, vmem_limit_bytes=56 * 1024 * 1024
        ),
    )(*args)


def solution(mesh):
    in_specs = (
        P(("groups", "grid"), None),
        P("grid", "feat"),
        P("grid", None, None),
        P("grid", None, None),
        P("grid"),
        P("grid"),
        P("grid", None, None),
        P("grid", None, None),
        P(None, "feat"),
        P(None, "feat"),
        P("feat"),
        P("feat", None),
        P("feat"),
        P(None, None, "feat"),
        P(None, None, "feat"),
        P(None, "feat"),
        P(None, "feat", None),
        P(None, "feat"),
        P(None, "feat"),
        P(None, "feat"),
        P("feat"),
        P("feat", None),
    )
    out_specs = P(("groups", "grid", "feat"), None)
    return jax.shard_map(local, mesh=mesh, in_specs=in_specs, out_specs=out_specs, check_vma=False)
```

time: 212 us -> 66.7 us (0.31)
  waiting for transfers between devices: 64.2 us -> 0 us
  Pallas kernels: 0 us -> 61.1 us
  blocking collectives: 57.9 us -> 0 us
  starting transfers between devices: 29.3 us -> 0 us
  matrix products: 27.8 us -> 0 us
  between operations: 13.5 us -> 0.01 us
  other arithmetic: 8.29 us -> 0 us
  local copies, waits for them, and re-layouts: 9.7 us -> 5.34 us
    pallas_call x0 -> x1, Pallas kernels: none -> 61.1 us  [local(): pl.pallas_call(functools.partial(kernel, n_grid, n_feat), out_shape=jax.S...]
    unnamed x6 -> x0, waiting for transfers between devices: 59.5 us -> none
    all_gather x5 -> x0, blocking collectives: 40.8 us -> none  [the longest x4 32.8 us: project(): shard_part = lax.all_gather(latent_bf, 'feat', axis=1, tiled=True)]
    dot_general x14 -> x0, matrix products: 27.8 us -> none  [the longest x2 9.48 us: local(): jnp.dot(one_hot(mesh_senders, widened.shape[0]), widened, preferred_eleme...]
    all_to_all x5 -> x0, starting transfers between devices: 22.5 us -> none  [the longest x2 8.81 us: local(): lax.all_to_all(outgoing, 'grid', split_axis=0, concat_axis=0, tiled=True)]
    psum x3 -> x0, blocking collectives: 17.1 us -> none  [update(): lax.psum((jnp.sum(blended, axis=1), jnp.sum(blended * blended, axis=1)),...]
    ppermute x4 -> x0, starting transfers between devices: 6.67 us -> none  [the longest x2 4.02 us: padded(): lax.ppermute(head, axis, [((i + 1) % count, i) for i in range(count)])]
    all_to_all x5 -> x0, waiting for transfers between devices: 4.66 us -> none  [the longest x2 4.61 us: local(): lax.all_to_all(outgoing, 'grid', split_axis=0, concat_axis=0, tiled=True)]
  transfers between devices with their start and end apart: 12 -> 0, of which waited for: 4 -> 0; matrix products, arithmetic and copies ran while one was open for 11% -> 0% of each run, Pallas kernels for 0% -> 0%
where the time goes in v1:
time: 66.7 us; the launch traced here: 66.5 us
  Pallas kernels  61.1 us (92%)
  local copies, waits for them, and re-layouts  5.34 us (8%)
    pallas_call x1, Pallas kernels, local(): pl.pallas_call(functools.partial(kernel, n_grid, n_feat), out_shape=jax.S...  61.1 us
    unnamed x2, local copies, waits for them, and re-layouts  3.57 us
    pallas_call x1, local copies, waits for them, and re-layouts, local(): pl.pallas_call(functools.partial(kernel, n_grid, n_feat), out_shape=jax.S...  1.77 us

profile of v1, /device:TPU:1, one launch (start us, length us, event | category | flops | bytes accessed | tf_op | source)
XLA Modules:
  0.0 66.5 jit_solution(837866072286391362)
XLA Ops:
  0.0 1.6 %copy.24.dec_out_w = bf16[128,227]{1,0:T(8,128)(2,1)} copy(bf16[128,227]{0,1:T(8,128)(2,1)} %param.43) | data formatting | bytes 116224 | tf_op args[21]
  1.6 2.0 %copy.23.grid_state = bf16[1024,227]{1,0:T(8,128)(2,1)} copy(bf16[1024,227]{0,1:T(8,128)(2,1)} %param.22) | data formatting | bytes 929792 | tf_op args[0]
  3.6 61.1 %shard_map.208 = f32[256,227]{1,0:T(8,128)} custom-call(bf16[1024,227]{1,0:T(8,128)(2,1)} %copy.23.grid_state, bf16[512,128]{1,0:T(8,128)(2,1)} %mesh_state.1, s32[1,4,32]{2,1,0:T(4,128)} %enc_rows.1, s32[1,4,32]{2,1,0:T(4,128)} %enc_targets.1, s32[32,128]{1,0:T(8,128)} %bitcast.5, s32[32,128]{1,0:T(8,128)} %bitcast.6, s32[1,4,64]{2,1,0:T(4,128)} %dec_rows.1, ...), custom_call_target="tpu_custom_call" | custom-call | tf_op jit(solution)/shard_map/pallas_call | solution.py:452
  64.7 1.8 %copy.25 = f32[256,227]{0,1:T(8,128)} copy(f32[256,227]{1,0:T(8,128)} %shard_map.208) | data formatting | bytes 464896 | tf_op jit(solution)/shard_map/pallas_call | solution.py:452

commit v2 on v1

--- a/solution.py
+++ b/solution.py
@@ -49,6 +49,10 @@
 
 def dot_t(a, b):
     return lax.dot_general(a, b, (((0,), (0,)), ((), ())), preferred_element_type=F32)
+
+
+def dot_n(a, b):
+    return lax.dot_general(a, b, (((1,), (1,)), ((), ())), preferred_element_type=F32)
 
 
 def silu(x):
@@ -115,7 +119,7 @@
     cross = (f + 2) % n_feat
     layers = proc_send_w.shape[0]
     nodes, part = mesh_state.shape
-    grid_rows = grid_state.shape[0]
+    variables, grid_rows = grid_state.shape
     cap, cap2 = enc_rows.shape[2], dec_rows.shape[2]
     edges = senders.shape[0] * EDGE_TILE
     sems = [0]
@@ -214,13 +218,15 @@
     out_w_all[0, columns(f), :] = enc_out_w[...]
     for layer in range(layers):
         out_w_all[1 + layer, columns(f), :] = proc_out_w[layer]
-    dec_w_all[columns(f), :] = dec_out_w[...]
-
+    dec_w_all[:, columns(f)] = jnp.zeros((dec_w_all.shape[0], part), BF)
+    dec_w_all[:variables, columns(f)] = dec_out_w[...]
+
+    block = 128
     state_gather = Gather(state_all, False, 2)
     gain_gather = Gather(gain_all, False, 1)
     weight_gathers = [Gather(out_w_all.at[i], True, 1) for i in range(1 + layers)]
-    dec_weight_gather = Gather(dec_w_all, True, 1)
-    sum_gathers = [Gather(sums_all.at[i], False, 4) for i in range(1 + layers)]
+    dec_weight_gather = Gather(dec_w_all, False, 1)
+    sum_gathers = [Gather(sums_all.at[i], False, nodes // block) for i in range(1 + layers)]
     dec_gather = Gather(dec_all, False, 2)
     enc_slots = Exchange(enc_out_slots, enc_in_slots, cap)
     enc_index = Exchange(enc_out_index, enc_in_index, cap)
@@ -230,15 +236,14 @@
     pl.semaphore_wait(barrier, 2 + n_grid - 1)
     state_gather.start()
 
-    def enc_send(b):
-        rows = as_column(enc_rows[0, pl.ds(b, 1), :])
-        picked = dot(hits(rows, grid_rows, 0), grid_state[...]).astype(BF)
-        where = pl.ds(pl.multiple_of(b * cap, cap), cap)
-        enc_out_slots[where, :] = dot(picked, enc_grid_w[...]).astype(BF)
-        target = as_column(enc_targets[0, pl.ds(b, 1), :])
-        enc_out_index[where, :] = jnp.broadcast_to(target, (cap, 128))
-
-    repeat(n_grid, enc_send)
+    grid_proj = dot_t(grid_state[...], enc_grid_w[...]).astype(BF)
+    for i in range(n_grid // 4):
+        parts = range(4 * i, 4 * i + 4)
+        where = pl.ds(i * 4 * cap, 4 * cap)
+        rows = jnp.concatenate([as_column(enc_rows[0, b : b + 1, :]) for b in parts], axis=0)
+        enc_out_slots[where, :] = dot(hits(rows, grid_rows, 0), grid_proj).astype(BF)
+        target = jnp.concatenate([as_column(enc_targets[0, b : b + 1, :]) for b in parts], axis=0)
+        enc_out_index[where, :] = jnp.broadcast_to(target, (4 * cap, 128))
     enc_slots.start()
     enc_index.start()
     gain_gather.start()
@@ -294,17 +299,16 @@
     sum_gathers[0].start()
     edge_tiles(tiles // 2, tiles)
 
-    block = 128
-
     def update(step):
         gather = sum_gathers[step]
         gather.middle()
         if step == 0:
             gain_gather.finish()
         weight_gathers[step].finish()
-        gather.finish()
+        gather.direct.wait_recv()
         for i in range(nodes // block):
             rows = slice(i * block, (i + 1) * block)
+            gather.forward[i].wait_recv()
             u = dot(sums_all[step, rows, :], out_w_all[step])
             centre = jnp.mean(u, axis=1, keepdims=True)
             spread = jnp.mean(u * u, axis=1, keepdims=True) - centre * centre
@@ -312,6 +316,7 @@
             held += gain_all[step : step + 1, :] * ((u - centre) * lax.rsqrt(spread + 1e-05))
             latent[rows, :] = held
             latent_bf[rows, :] = held.astype(BF)
+        sent.extend([gather.direct] + gather.over + gather.forward)
 
     update(0)
     right, left = (z + 1) % n_grid, (z + n_grid - 1) % n_grid
@@ -354,7 +359,7 @@
         sent.extend([up, down])
         if layer == 0:
             dec_index.finish()
-            query = dot(grid_state[...], dec_grid_w[...]).astype(BF)
+            query = dot_t(grid_state[...], dec_grid_w[...]).astype(BF)
             quarter = grid_rows // n_feat
             for i in range(n_grid // 4):
                 where = pl.ds(i * 4 * cap2, 4 * cap2)
@@ -382,8 +387,9 @@
     for i in range(n_grid // 4):
         where = pl.ds(i * 4 * cap2, 4 * cap2)
         total += dot_t(dec_spread[where, :], dec_all[where, :])
-    own = grid_state[pl.ds(pl.multiple_of(f * quarter, quarter), quarter), :]
-    out[...] = own.astype(F32) + dot(total.astype(BF), dec_w_all[...])
+    own = grid_state[:, pl.ds(pl.multiple_of(f * quarter, quarter), quarter)]
+    added = dot_n(dec_w_all[...], total.astype(BF))
+    out[...] = own.astype(F32) + added[:variables, :]
 
     for copy in sent:
         copy.wait_send()
@@ -426,7 +432,7 @@
     quarter = grid_rows // n_feat
     sems = 9 * 12 + 2 * layers + 4 * n_grid
     args = (
-        grid_state,
+        grid_state.T,
         mesh_state,
         enc_rows,
         enc_targets,
@@ -447,18 +453,18 @@
         dec_mesh_w,
         dec_grid_w,
         dec_bias.reshape(1, -1),
-        dec_out_w,
+        dec_out_w.T,
     )
     return pl.pallas_call(
         functools.partial(kernel, n_grid, n_feat),
-        out_shape=jax.ShapeDtypeStruct((quarter, variables), F32),
+        out_shape=jax.ShapeDtypeStruct((variables, quarter), F32),
         in_specs=[pl.BlockSpec(memory_space=pltpu.VMEM)] * len(args),
         out_specs=pl.BlockSpec(memory_space=pltpu.VMEM),
         scratch_shapes=[
             pltpu.VMEM((nodes, width), BF),
             pltpu.VMEM((8, width), F32),
             pltpu.VMEM((1 + layers, width, width), BF),
-            pltpu.VMEM((width, variables), BF),
+            pltpu.VMEM((-(-variables // 16) * 16, width), BF),
             pltpu.VMEM((1 + layers, nodes, width), BF),
             pltpu.VMEM((dec_total, width), BF),
             pltpu.VMEM((enc_total, part), BF),
@@ -485,7 +491,7 @@
         compiler_params=pltpu.CompilerParams(
             collective_id=0, has_side_effects=True, vmem_limit_bytes=56 * 1024 * 1024
         ),
-    )(*args)
+    )(*args).T
 
 
 def solution(mesh):

time: 66.7 us -> 62.2 us (0.933)
  local copies, waits for them, and re-layouts: 5.34 us -> 1.65 us
  Pallas kernels: 61.1 us -> 60.4 us
    unnamed x2 -> x1, local copies, waits for them, and re-layouts: 3.57 us -> 1.65 us
    pallas_call x1 -> x0, local copies, waits for them, and re-layouts: 1.77 us -> none  [local(): pl.pallas_call(functools.partial(kernel, n_grid, n_feat), out_shape=jax.S...]
    pallas_call x1, Pallas kernels: 61.1 us -> 60.4 us  [local(): pl.pallas_call(functools.partial(kernel, n_grid, n_feat), out_shape=jax.S...]
where the time goes in v2:
time: 62.2 us; the launch traced here: 62.1 us
  Pallas kernels  60.4 us (97%)
  local copies, waits for them, and re-layouts  1.65 us (3%)
    pallas_call x1, Pallas kernels, local(): pl.pallas_call(functools.partial(kernel, n_grid, n_feat), out_shape=jax.S...  60.4 us
    unnamed x1, local copies, waits for them, and re-layouts  1.65 us

profile of v2, /device:TPU:1, one launch (start us, length us, event | category | flops | bytes accessed | tf_op | source)
XLA Modules:
  0.0 62.1 jit_solution(9900720997831737056)
XLA Ops:
  0.0 60.4 %shard_map.208 = f32[227,256]{1,0:T(8,128)} custom-call(bf16[227,1024]{1,0:T(8,128)(2,1)} %bitcast.9, bf16[512,128]{1,0:T(8,128)(2,1)} %mesh_state.1, s32[1,4,32]{2,1,0:T(4,128)} %enc_rows.1, s32[1,4,32]{2,1,0:T(4,128)} %enc_targets.1, s32[32,128]{1,0:T(8,128)} %bitcast.11, s32[32,128]{1,0:T(8,128)} %bitcast.12, s32[1,4,64]{2,1,0:T(4,128)} %dec_rows.1, ...), custom_call_target="tpu_custom_call" | custom-call | tf_op jit(solution)/shard_map/pallas_call | solution.py:458
  60.4 1.6 %copy.24 = f32[256,227]{0,1:T(8,128)} copy(f32[256,227]{0,1:T(8,128)} %bitcast.8) | data formatting | bytes 464896

commit v3 on v2

--- a/solution.py
+++ b/solution.py
@@ -280,8 +280,6 @@
 
     tiles = edges // EDGE_TILE
     edge_tiles(0, tiles // 2)
-    gain_gather.middle()
-    weight_gathers[0].middle()
 
     state_gather.finish()
     mesh_proj = dot(state_all[...], enc_mesh_w[...]).astype(BF)
@@ -297,6 +295,8 @@
         total += dot_t(select, silu(before).astype(BF))
     sums_all[0, :, columns(f)] = total.astype(BF)
     sum_gathers[0].start()
+    gain_gather.middle()
+    weight_gathers[0].middle()
     edge_tiles(tiles // 2, tiles)
 
     def update(step):
@@ -345,9 +345,6 @@
             pre[rows, :] = dot(gather_sel[rows, : 2 * nodes], table[layer])
         up.wait_recv()
         down.wait_recv()
-        weight_gathers[1 + layer].middle()
-        if layer == layers - 1:
-            dec_weight_gather.middle()
         total = jnp.zeros((nodes, part), F32)
         for i in range(edges // EDGE_BLOCK):
             rows = slice(i * EDGE_BLOCK, (i + 1) * EDGE_BLOCK)
@@ -356,6 +353,9 @@
             total += dot(scatter_sel[:, rows], hidden)
         sums_all[1 + layer, :, columns(f)] = total.astype(BF)
         sum_gathers[1 + layer].start()
+        weight_gathers[1 + layer].middle()
+        if layer == layers - 1:
+            dec_weight_gather.middle()
         sent.extend([up, down])
         if layer == 0:
             dec_index.finish()

time: 62.2 us -> 58.8 us (0.945)
  Pallas kernels: 60.4 us -> 56.9 us
    pallas_call x1, Pallas kernels: 60.4 us -> 56.9 us  [local(): pl.pallas_call(functools.partial(kernel, n_grid, n_feat), out_shape=jax.S...]
where the time goes in v3:
time: 58.8 us; the launch traced here: 58.6 us
  Pallas kernels  56.9 us (97%)
  local copies, waits for them, and re-layouts  1.65 us (3%)
    pallas_call x1, Pallas kernels, local(): pl.pallas_call(functools.partial(kernel, n_grid, n_feat), out_shape=jax.S...  56.9 us
    unnamed x1, local copies, waits for them, and re-layouts  1.65 us

profile of v3, /device:TPU:1, one launch (start us, length us, event | category | flops | bytes accessed | tf_op | source)
XLA Modules:
  0.0 58.6 jit_solution(9199533450025845630)
XLA Ops:
  0.0 56.9 %shard_map.208 = f32[227,256]{1,0:T(8,128)} custom-call(bf16[227,1024]{1,0:T(8,128)(2,1)} %bitcast.9, bf16[512,128]{1,0:T(8,128)(2,1)} %mesh_state.1, s32[1,4,32]{2,1,0:T(4,128)} %enc_rows.1, s32[1,4,32]{2,1,0:T(4,128)} %enc_targets.1, s32[32,128]{1,0:T(8,128)} %bitcast.11, s32[32,128]{1,0:T(8,128)} %bitcast.12, s32[1,4,64]{2,1,0:T(4,128)} %dec_rows.1, ...), custom_call_target="tpu_custom_call" | custom-call | tf_op jit(solution)/shard_map/pallas_call | solution.py:458
  56.9 1.6 %copy.24 = f32[256,227]{0,1:T(8,128)} copy(f32[256,227]{0,1:T(8,128)} %bitcast.8) | data formatting | bytes 464896
